TPU v7x, 128 devices: a whole 4x4x4 slice. The times are simulated.
128 devices in a mesh: doc: 4 (over z), seq: 32 (over y, x, core).
Axes of the slice: x: 4, y: 4, z: 4, core: 2. Of those that a mesh axis runs over, the one named last changes fastest.
Arguments:
- text: bfloat16 [16384, 4096], P(('doc', 'seq')), may hold values from -6 to 6
- norm_gain: float32 [4096], replicated, may hold values from 0.1 to 1.9
- q_weight: bfloat16 [4096, 2048], P('seq'), may hold values from -0.09375 to 0.09375
- k_weight: bfloat16 [4096, 512], P('seq'), may hold values from -0.09375 to 0.09375
- v_weight: bfloat16 [4096, 512], P('seq'), may hold values from -0.09375 to 0.09375
- q_gain: float32 [128], replicated, may hold values from 1.4 to 7
- k_gain: float32 [128], replicated, may hold values from 1.4 to 7
- vision: bfloat16 [128, 1601, 4096], P(('doc', 'seq')), may hold values from -6 to 6
- tiles_per_image: int32 [4, 2], replicated, may hold values from 0 to 4, as said below
- image_start: int32 [4, 2], replicated, may hold values from 0 to 4096, as said below
- tile_owner: int32 [4, 4], replicated, may hold values from 0 to 31, as said below
Outputs:
- context: bfloat16 [16384, 2048], P(('doc', 'seq'))
Inputs may be any that keep to these rules, and one draw needn't show every extreme that they name: `tiles_per_image`: A document's present images come first, each with 1 or more tiles, and the absent ones have 0; each document has 1 to 2 present images; some document has exactly 1 image and some other has 2; a document's tiles sum to at most 4, and some document has exactly 4. `image_start`: strictly increasing over a document's present images; images with 0 tiles start at 4096. `tile_owner`: the 4 entries of a document are distinct.
All inputs are finite; a program needn't handle non-finite values.
Results may differ from a plain program's by a relative error of at most 0.006.
The roundings to bfloat16 on the way count: a program that leaves them out, or rounds other values in their place, can miss the bound.
Values may be sent and summed in bfloat16 or wider, within the bound.
No kernel may reach another device: no remote copies, remote signals or barrier semaphores. Data moves between devices by JAX's collectives and lax.ppermute only.
A program may use at most 256 MiB of HBM per device.

v0:
```python
import functools

import jax
import jax.numpy as jnp
from jax import lax
from jax.experimental import pallas as pl
from jax.experimental.pallas import tpu as pltpu
from jax.sharding import Mesh
from jax.sharding import PartitionSpec as P

SEQ = ("y", "x", "c")
PLANE = ("y", "x")
PARTS = 8
ROWS = 208
HALF = 4 * ROWS
NONE = -1e30
MASKED = -2e30
LOG2E = 1.4426950408889634


def tile_spans(tile_counts, starts, length, most_tiles):
    slots = tile_counts.shape[0]
    span_ends = jnp.concatenate([starts[1:], jnp.full((1,), length, jnp.int32)])
    offsets = jnp.cumsum(tile_counts) - tile_counts
    tile_total = jnp.sum(tile_counts)
    tile_ids = jnp.arange(most_tiles, dtype=jnp.int32)
    image_of = jnp.sum((offsets[None, :] <= tile_ids[:, None]).astype(jnp.int32), axis=1) - 1
    member = jnp.arange(slots, dtype=jnp.int32)[None, :] == image_of[:, None]
    tile_low = jnp.sum(jnp.where(member, starts[None, :], 0), axis=1)
    tile_high = jnp.sum(jnp.where(member, span_ends[None, :], 0), axis=1)
    return (tile_low, tile_high, tile_ids < tile_total)


def ring(step):
    return [(i, (i + step) % 4) for i in range(4)]


def norm_rows(values, gain):
    return values * lax.rsqrt(jnp.mean(values * values, axis=-1, keepdims=True) + 1e-05) * gain


CHUNKS = ((0, 512), (512, 1024), (1024, 2048), (2048, 3072), (3072, 4096))


def kv_kernel(
    tile_len, meta_ref, own_ref, other_ref, own_tail, other_tail, weight_ref, gain_ref, out_ref,
    tile_buf, weight_buf, acc_ref, tile_sem, tail_sem, weight_sem,
):
    core, own = meta_ref[0], meta_ref[1]
    whole = tile_len // 16 * 16 - HALF
    kv_width = weight_buf.shape[1]

    def weight_copy(k):
        low, high = CHUNKS[k]
        at = pl.ds(low, high - low)
        return pltpu.make_async_copy(weight_ref.at[at, pl.ds(0, kv_width)], weight_buf.at[at], weight_sem.at[k])

    def tile_copies(k, source, tail, lower):
        low, high = CHUNKS[k]
        at = pl.ds(low, high - low)
        if not lower:
            rows = pl.ds(0, HALF)
            return [pltpu.make_async_copy(source.at[rows, at], tile_buf.at[rows, at], tile_sem.at[k])]
        return [
            pltpu.make_async_copy(
                source.at[pl.ds(HALF, whole), at], tile_buf.at[pl.ds(0, whole), at], tile_sem.at[k]
            ),
            pltpu.make_async_copy(tail.at[:, at], tile_buf.at[pl.ds(whole, 16), at], tail_sem.at[k]),
        ]

    for k in range(len(CHUNKS)):
        weight_copy(k).start()
        for from_own, source, tail in ((1, own_ref, own_tail), (0, other_ref, other_tail)):
            for lower in (0, 1):

                @pl.when((own == from_own) & (core == lower))
                def _(k=k, source=source, tail=tail, lower=lower):
                    for copy in tile_copies(k, source, tail, lower):
                        copy.start()

    for k, (low, high) in enumerate(CHUNKS):
        weight_copy(k).wait()
        for lower in (0, 1):

            @pl.when(core == lower)
            def _(k=k, lower=lower):
                for copy in tile_copies(k, own_ref, own_tail, lower):
                    copy.wait()

        part = jnp.dot(tile_buf[:, low:high], weight_buf[low:high, :], preferred_element_type=jnp.float32)
        if k == 0:
            acc_ref[...] = part
        else:
            acc_ref[...] += part

    for y in range(4):
        held = tile_len - core * HALF - y * ROWS
        kept = lax.broadcasted_iota(jnp.int32, (ROWS, 128), 0) < held
        for h in range(4):
            at = slice(y * ROWS, (y + 1) * ROWS)
            keys = acc_ref[at, h * 128 : (h + 1) * 128]
            values = acc_ref[at, (h + 4) * 128 : (h + 5) * 128]
            if y == 3:
                keys, values = jnp.where(kept, keys, 0.0), jnp.where(kept, values, 0.0)
            out_ref[y * 4 + h, :, :128] = norm_rows(keys, gain_ref[...]).astype(jnp.bfloat16)
            out_ref[y * 4 + h, :, 128:] = values.astype(jnp.bfloat16)


def ragged_end(tile):
    whole = tile.shape[0] // 16 * 16
    return jnp.pad(tile[whole:], ((0, 16 - tile.shape[0] + whole), (0, 0)))


def project_kv(own, other, tails, weights, k_gain, core, use_own):
    tile_len, depth = own.shape
    width = 1024
    meta = jnp.stack([core, use_own]).astype(jnp.int32)
    chunks = len(CHUNKS)
    return pl.pallas_call(
        functools.partial(kv_kernel, tile_len),
        in_specs=[pl.BlockSpec(memory_space=pltpu.SMEM)]
        + [pl.BlockSpec(memory_space=pl.ANY)] * 5
        + [pl.BlockSpec(memory_space=pltpu.VMEM)],
        out_specs=pl.BlockSpec(memory_space=pltpu.VMEM),
        out_shape=jax.ShapeDtypeStruct((16, ROWS, 256), jnp.bfloat16),
        scratch_shapes=[
            pltpu.VMEM((HALF, depth), jnp.bfloat16),
            pltpu.VMEM((depth, width), jnp.bfloat16),
            pltpu.VMEM((HALF, width), jnp.float32),
            pltpu.SemaphoreType.DMA((chunks,)),
            pltpu.SemaphoreType.DMA((chunks,)),
            pltpu.SemaphoreType.DMA((chunks,)),
        ],
        compiler_params=pltpu.CompilerParams(vmem_limit_bytes=40 * 2**20),
        cost_estimate=pl.CostEstimate(
            flops=2 * HALF * depth * width, bytes_accessed=2 * (HALF + width) * depth, transcendentals=0
        ),
        name="kv_projection",
    )(meta, own, other, *tails, weights, k_gain)


def attend_kernel(pad, meta_ref, q_ref, *refs):
    part_refs, (out_ref, m_ref, l_ref, acc_ref) = refs[:-4], refs[-4:]
    tile = pl.program_id(0)
    blocks, rows, width = q_ref.shape
    heads = width // 128
    keys = PARTS * ROWS
    factor = LOG2E / 128**0.5
    pairs = heads // 2

    @pl.when(tile == 0)
    def _():
        m_ref[...] = jnp.full_like(m_ref, NONE)
        l_ref[...] = jnp.zeros_like(l_ref)
        acc_ref[...] = jnp.zeros_like(acc_ref)

    low, high = meta_ref[tile], meta_ref[4 + tile]
    some, every = False, True
    for b in range(blocks):
        first = meta_ref[8 + b]
        some = some | ((low < first + rows) & (high > first))
        every = every & (low <= first) & (high >= first + rows)

    def step(partial):
        held = []
        for own, before, after, low_tiles, high_tiles in (part_refs[:5], part_refs[5:]):
            opposite = jnp.where(tile < 2, low_tiles[0], high_tiles[0])
            held += [own[0], before[0], after[0], opposite]
        kv = jnp.concatenate(held, axis=0)
        row = lax.broadcasted_iota(jnp.int32, (keys, 128), 0)
        padding = (row >= meta_ref[8 + blocks]) & (row < meta_ref[8 + blocks] + pad)
        lane = lax.broadcasted_iota(jnp.int32, (keys, 128), 1) == 0
        bias = jnp.where(padding & lane, MASKED, 0.0).astype(jnp.bfloat16)
        key = jnp.concatenate([kv[:, :128], bias], axis=1)
        value = jnp.concatenate([kv[:, 128:], jnp.ones((keys, 128), jnp.bfloat16)], axis=1)
        one = (lax.broadcasted_iota(jnp.int32, (2 * rows, 128), 1) == 0).astype(jnp.bfloat16)

        def score(group):
            b, h = group // pairs, group % pairs * 2
            both = [q_ref[b, :, i * 128 : (i + 1) * 128] for i in (h, h + 1)]
            deep = jnp.concatenate([jnp.concatenate(both, axis=0), one], axis=1)
            return lax.dot_general(deep, key, (((1,), (1,)), ((), ())), preferred_element_type=jnp.float32)

        def soften(group, scores):
            if partial:
                at = meta_ref[8 + group // pairs] + lax.broadcasted_iota(jnp.int32, (2 * rows, 1), 0) % rows
                scores = jnp.where((at >= low) & (at < high), scores, MASKED)
            m_old = m_ref[group]
            m_new = jnp.maximum(m_old, jnp.max(scores, axis=1, keepdims=True))
            probs = jnp.exp2((scores - m_new) * factor)
            alpha = jnp.exp2((m_old - m_new) * factor)
            m_ref[group] = m_new
            summed = jnp.dot(probs.astype(jnp.bfloat16), value, preferred_element_type=jnp.float32)
            l_ref[group] = l_ref[group] * alpha + summed[:, 128:129]
            acc_ref[group] = acc_ref[group] * alpha + summed[:, :128]

        scores = score(0)
        for group in range(blocks * pairs):
            ahead = score(group + 1) if group + 1 < blocks * pairs else None
            soften(group, scores)
            scores = ahead

    pl.when(every)(lambda: step(False))
    pl.when(some & jnp.logical_not(every))(lambda: step(True))

    @pl.when(tile == pl.num_programs(0) - 1)
    def _():
        for b in range(blocks):
            for h in range(heads):
                group, at = b * pairs + h // 2, slice(h % 2 * rows, (h % 2 + 1) * rows)
                out_ref[b, :, h * 128 : (h + 1) * 128] = (
                    acc_ref[group, at] / jnp.maximum(l_ref[group, at], 1.0)
                ).astype(jnp.bfloat16)


def attend(query, parts, meta, pad):
    blocks, rows, width = query.shape
    tiles = parts[0].shape[0]
    groups = blocks * width // 256
    return pl.pallas_call(
        functools.partial(attend_kernel, pad),
        grid_spec=pltpu.PrefetchScalarGridSpec(
            num_scalar_prefetch=1,
            grid=(tiles,),
            in_specs=[
                pl.BlockSpec((blocks, rows, width), lambda j, meta: (0, 0, 0)),
            ]
            + (
                [pl.BlockSpec((1, ROWS, 256), lambda j, meta: (j, 0, 0))] * 3
                + [pl.BlockSpec((1, ROWS, 256), lambda j, meta: (jnp.minimum(j, 1), 0, 0))]
                + [pl.BlockSpec((1, ROWS, 256), lambda j, meta: (jnp.maximum(j - 2, 0), 0, 0))]
            )
            * 2,
            out_specs=pl.BlockSpec((blocks, rows, width), lambda j, meta: (0, 0, 0)),
            scratch_shapes=[
                pltpu.VMEM((groups, 2 * rows, 1), jnp.float32),
                pltpu.VMEM((groups, 2 * rows, 1), jnp.float32),
                pltpu.VMEM((groups, 2 * rows, 128), jnp.float32),
            ],
        ),
        out_shape=jax.ShapeDtypeStruct(query.shape, jnp.bfloat16),
        compiler_params=pltpu.CompilerParams(vmem_limit_bytes=40 * 2**20),
        cost_estimate=pl.CostEstimate(
            flops=8 * blocks * rows * width * tiles * PARTS * ROWS,
            bytes_accessed=512 * tiles * PARTS * ROWS,
            transcendentals=blocks * rows * width // 128 * tiles * PARTS * ROWS,
        ),
        name="attention",
    )(meta, query, *parts)


def query_kernel(text0, text1, text2, text3, weight_ref, gain_ref, out_ref, acc_ref):
    step = pl.program_id(0)
    text = jnp.concatenate([ref[...] for ref in (text0, text1, text2, text3)], axis=0)
    part = jnp.dot(text, weight_ref[...], preferred_element_type=jnp.float32)

    @pl.when(step == 0)
    def _():
        acc_ref[...] = part

    @pl.when(step > 0)
    def _():
        acc_ref[...] += part

    @pl.when(step == pl.num_programs(0) - 1)
    def _():
        for b in range(4):
            for h in range(acc_ref.shape[1] // 128):
                block = acc_ref[b * 128 : (b + 1) * 128, h * 128 : (h + 1) * 128]
                out_ref[b, :, h * 128 : (h + 1) * 128] = norm_rows(block, gain_ref[...]).astype(jnp.bfloat16)


def project_query(texts, weights, gain):
    rows, depth = texts[0].shape
    width = 512
    chunk = 1024
    last = weights.shape[1] // width - 1
    return pl.pallas_call(
        query_kernel,
        grid=(depth // chunk,),
        in_specs=[pl.BlockSpec((rows, chunk), lambda i: (0, i))] * 4
        + [pl.BlockSpec((chunk, width), lambda i: (i, last)), pl.BlockSpec((1, 128), lambda i: (0, 0))],
        out_specs=pl.BlockSpec((4, rows, width), lambda i: (0, 0, 0)),
        out_shape=jax.ShapeDtypeStruct((4, rows, width), jnp.bfloat16),
        scratch_shapes=[pltpu.VMEM((4 * rows, width), jnp.float32)],
        compiler_params=pltpu.CompilerParams(vmem_limit_bytes=32 * 2**20),
        cost_estimate=pl.CostEstimate(
            flops=8 * rows * depth * width, bytes_accessed=2 * (4 * rows + width) * depth, transcendentals=0
        ),
        name="query_projection",
    )(*texts, weights, gain)


def local(
    text,
    norm_gain,
    q_weight,
    k_weight,
    v_weight,
    q_gain,
    k_gain,
    vision,
    tiles_per_image,
    image_start,
    tile_owner,
):
    row_count = text.shape[0]
    head_dim = q_gain.shape[0]
    heads_kv = k_weight.shape[1] // head_dim
    tile_rows = vision[0]
    tile_len = tile_rows.shape[0]
    most_tiles = tile_owner.shape[1]
    length = row_count * lax.axis_size(SEQ)
    at_doc, at_y, at_x, at_core = (lax.axis_index(a) for a in ("z", "y", "x", "c"))

    group_width = q_weight.shape[1] // heads_kv
    q_share = lax.dynamic_slice_in_dim(q_weight, at_doc * group_width, group_width, 1)
    weights = lax.all_gather(jnp.concatenate([k_weight, v_weight, q_share], axis=1), SEQ, axis=0, tiled=True)
    other_rows = lax.ppermute(tile_rows, "c", [(0, 1), (1, 0)])
    text_wide = text.astype(jnp.float32)
    normed = norm_rows(text_wide, norm_gain).astype(jnp.bfloat16)
    around = [normed] + [
        lax.ppermute(normed, "z", ring(step)) for step in (1, 2, 3)
    ]
    tails = (ragged_end(tile_rows), ragged_end(other_rows))
    weights, other_rows, tails, *around = lax.optimization_barrier((weights, other_rows, tails, *around))

    totals = jnp.sum(tiles_per_image, axis=1)
    valid = jnp.arange(most_tiles, dtype=jnp.int32)[None, :] < totals[:, None]
    owned = jnp.any(
        (tile_owner[:, :, None] == jnp.arange(lax.axis_size(SEQ), dtype=jnp.int32)) & valid[:, :, None], axis=1
    )
    owned = owned.reshape(owned.shape[0], -1, 2)
    crowded = jnp.any(owned[:, :, 0] & owned[:, :, 1])
    picked = jnp.arange(tiles_per_image.shape[0], dtype=jnp.int32) == at_doc
    tile_counts = jnp.sum(jnp.where(picked[:, None], tiles_per_image, 0), axis=0)
    starts = jnp.sum(jnp.where(picked[:, None], image_start, 0), axis=0)
    owners = jnp.sum(jnp.where(picked[:, None], tile_owner, 0), axis=0)
    first_core = jnp.any(owned & picked[:, None, None], axis=0)[:, 0]
    tile_low, tile_high, tile_valid = tile_spans(tile_counts, starts, length, most_tiles)
    tile_low = jnp.where(tile_valid, tile_low, 2 * length)
    tile_high = jnp.where(tile_valid, tile_high, 0)

    chip_first = jnp.sum(
        jnp.where(jnp.arange(first_core.shape[0]) == at_y * 4 + at_x, first_core.astype(jnp.int32), 0)
    )
    source = 1 - chip_first
    gain_row = k_gain.reshape(1, head_dim)
    chip_of = owners // 2
    turn = jnp.where((owners % 2 == 1) & first_core[chip_of], 1, 0)

    def project(from_core):
        use_own = (at_core == from_core).astype(jnp.int32)
        return project_kv(tile_rows, other_rows, tails, weights, gain_row, at_core, use_own)

    pieces, weights = lax.optimization_barrier((project(source), weights))

    def send(sent):
        return lax.all_to_all(sent, PLANE, 0, 0, tiled=True)

    def pick(got):
        return jnp.stack([got[chip_of[j]] for j in range(most_tiles)])

    def ask():
        query = project_query(around, weights, q_gain.reshape(1, head_dim))
        return jnp.stack([query[0]] + [lax.ppermute(query[k], "z", ring(-k)) for k in (1, 2, 3)])

    def spread_one():
        got, mine = lax.optimization_barrier((send(pieces), ask()))
        return pick(got), mine

    def spread_two():
        got, second = lax.optimization_barrier((send(pieces), project(1)))
        later, mine = lax.optimization_barrier((send(second), ask()))
        return jnp.where((turn > 0)[:, None, None], pick(later), pick(got)), mine

    chosen, mine = lax.cond(crowded, spread_two, spread_one)

    after, before, swap = ring(1), ring(-1), [(0, 1), (1, 0)]
    from_before, from_after = lax.ppermute(chosen, "y", after), lax.ppermute(chosen, "y", before)
    half = most_tiles // 2
    opposite = [lax.ppermute(from_before[:half], "y", after), lax.ppermute(from_after[half:], "y", before)]
    parts = [chosen, from_before, from_after, *opposite]
    parts += [lax.ppermute(part, "c", swap) for part in parts]
    query = [mine[(at_x + s - at_doc) % 4] for s in range(4)]
    query = [query[0]] + [lax.ppermute(query[s], "x", ring(s)) for s in (1, 2, 3)]
    last_slot = jnp.array([1, 3, 2, 0], jnp.int32)[at_y]
    last_part = jnp.where(at_core == 1, last_slot, last_slot + 4)
    pad = 2 * HALF - tile_len
    pad_row = (last_part + 1) * ROWS - pad

    token_x = (at_x - jnp.arange(4, dtype=jnp.int32)) % 4
    blocks = ((at_y * 4 + token_x) * 2 + at_core) * row_count
    spans = jnp.concatenate([tile_low, tile_high])
    context = attend(jnp.stack(query), parts, jnp.concatenate([spans, blocks, pad_row[None]]), pad)
    context = [context[0]] + [lax.ppermute(context[k], "x", ring(-k)) for k in (1, 2, 3)]
    context = jnp.stack(context)
    return jnp.concatenate([context[(h - at_x) % 4] for h in range(heads_kv)], axis=1)


def solution(mesh):
    grid = Mesh(mesh.devices.reshape(4, 4, 4, 2), ("z", "y", "x", "c"))
    rows = ("z", "y", "x", "c")
    return jax.shard_map(
        local,
        mesh=grid,
        in_specs=(
            P(rows, None),
            P(),
            P(SEQ, None),
            P(SEQ, None),
            P(SEQ, None),
            P(),
            P(),
            P(rows, None, None),
            P(),
            P(),
            P(),
        ),
        out_specs=P(rows, None),
        check_vma=False,
    )
```

profile of v0, /device:TPU:33, one launch (start us, length us, event | category | flops | bytes accessed | tf_op | source)
XLA Modules:
  0.0 184.6 jit_solution(14069289199123637071)
XLA Ops:
  7.6 1.8 pad_maximum_fusion.6
  10.8 1.7 collective-permute-start.7
  13.7 2.0 %collective-permute-start.9 = (bf16[128,4096]{1,0:T(8,128)(2,1)S(1)}, bf16[128,4096]{1,0:T(8,128)(2,1)}, u32[]{:S(2)}, u32[]{:S(2)}) collective-permute-start(bf16[128,4096]{1,0:T(8,128)(2,1)S(1)} %fusion.4), channel_id=1, source_target_pairs={{0,96},{32,0},{64,32},{96,64},{1,97},{33,1},{65,33},{97,65},{2,98}... | collective-permute-start | bytes 3145736 | tf_op jit(solution)/shard_map/ppermute | solution.py:323
  24.1 6.1 %collective-permute-done.6.other_ref = bf16[1601,4096]{1,0:T(8,128)(2,1)} collective-permute-done((bf16[1601,4096]{1,0:T(8,128)(2,1)}, bf16[1601,4096]{1,0:T(8,128)(2,1)}, u32[]{:S(2)}, u32[]{:S(2)}) %collective-permute-start.6) | collective-permute-done | bytes 13115424 | tf_op jit(solution)/shard_map/ppermute | solution.py:319
  31.0 4.7 %collective-permute-done.7 = bf16[128,4096]{1,0:T(8,128)(2,1)S(1)} collective-permute-done((bf16[128,4096]{1,0:T(8,128)(2,1)S(1)}, bf16[128,4096]{1,0:T(8,128)(2,1)S(1)}, u32[]{:S(2)}, u32[]{:S(2)}) %collective-permute-start.7) | collective-permute-done | bytes 1048608 | tf_op jit(solution)/shard_map/ppermute | solution.py:323
  35.8 2.9 %collective-permute-done.8 = bf16[128,4096]{1,0:T(8,128)(2,1)} collective-permute-done((bf16[128,4096]{1,0:T(8,128)(2,1)S(1)}, bf16[128,4096]{1,0:T(8,128)(2,1)}, u32[]{:S(2)}, u32[]{:S(2)}) %collective-permute-start.8) | collective-permute-done | bytes 1048608 | tf_op jit(solution)/shard_map/ppermute | solution.py:323
  38.6 22.4 %collective-permute-done.9 = bf16[128,4096]{1,0:T(8,128)(2,1)} collective-permute-done((bf16[128,4096]{1,0:T(8,128)(2,1)S(1)}, bf16[128,4096]{1,0:T(8,128)(2,1)}, u32[]{:S(2)}, u32[]{:S(2)}) %collective-permute-start.9) | collective-permute-done | bytes 1048608 | tf_op jit(solution)/shard_map/ppermute | solution.py:323
  61.0 13.9 %all-gather.2.cloned.1.call-done.weight_ref = bf16[4096,1536]{1,0:T(8,128)(2,1)} async-done(((bf16[128,1536]{1,0:T(8,128)(2,1)}), bf16[4096,1536]{1,0:T(8,128)(2,1)}) %all-gather.2.cloned.1.call-update) | async-done | bytes 12582928 | tf_op jit(solution)/shard_map/all_gather | solution.py:318
  74.9 11.3 %kv_projection.3 = bf16[16,208,256]{2,1,0:T(8,128)(2,1)} custom-call(s32[2]{0:T(128)S(1)} %pad_add_fusion.3.meta_ref, bf16[1601,4096]{1,0:T(8,128)(2,1)} %bitcast.71, bf16[1601,4096]{1,0:T(8,128)(2,1)} %collective-permute-done.6.other_ref, bf16[16,4096]{1,0:T(8,128)(2,1)S(1)} %pad.7.own_tail, bf16[16,4096]{1,0:T(8,128)(2,1)S(1)} %pad.8.other_tail, ...), custom_call_target="tpu_custom_call" | custom-call | flops 6979321856 | bytes 15204352 | tf_op jit(solution)/shard_map/kv_projection/pallas_call | solution.py:119
  86.2 33.4 %conditional.1 = (bf16[4,208,256]{2,1,0:T(8,128)(2,1)}, bf16[4,128,512]{2,1,0:T(8,128)(2,1)S(1)}) conditional(s32[]{:T(128)} %convert_element_type.21, (bf16[16,208,256]{2,1,0:T(8,128)(2,1)}, f32[128]{0:T(128)S(1)}, bf16[128,4096]{1,0:T(8,128)(2,1)S(1)}, bf16[128,4096]{1,0:T(8,128)(2,1)S(1)}, bf16[128,4096]{1,0:T(8,128)(2,1)}, ...), branch_computations={%region_14.15_spmd, %region_15.16_spmd} | conditional | flops 9129083904 | bytes 40473188 | solution.py:377
  86.2 4.9 %all-to-all-start = ((bf16[16,208,256]{2,1,0:T(8,128)(2,1)}), bf16[16,208,256]{2,1,0:T(8,128)(2,1)}, u32[]{:S(2)}, u32[]{:S(2)}) async-start(bf16[16,208,256]{2,1,0:T(8,128)(2,1)} %get-tuple-element.113), calls=%async_computation | async-start | bytes 3407872 | tf_op jit(solution)/shard_map/cond/branch_0_fun/all_to_all | solution.py:359
  91.1 5.8 %query_projection.2 = bf16[4,128,512]{2,1,0:T(8,128)(2,1)S(1)} custom-call(bf16[128,4096]{1,0:T(8,128)(2,1)S(1)} %get-tuple-element.114.text0, bf16[128,4096]{1,0:T(8,128)(2,1)S(1)} %get-tuple-element.115.text1, bf16[128,4096]{1,0:T(8,128)(2,1)} %get-tuple-element.116.text2, bf16[128,4096]{1,0:T(8,128)(2,1)} %get-tuple-element.117.text3, ...), custom_call_target="tpu_custom_call" | custom-call | flops 2147483648 | bytes 8388608 | tf_op jit(solution)/shard_map/cond/branch_0_fun/query_projection/pallas_call | solution.py:278
  97.0 1.3 collective-permute-start.2
  99.1 2.0 %collective-permute-start = (bf16[128,512]{1,0:T(8,128)(2,1)S(1)}, bf16[128,512]{1,0:T(8,128)(2,1)S(1)}, u32[]{:S(2)}, u32[]{:S(2)}) collective-permute-start(bf16[128,512]{1,0:T(8,128)(2,1)S(1)} %get-tuple-element.198), channel_id=1, source_target_pairs={{0,96},{32,0},{64,32},{96,64},{1,97},{33,1},{65,33},{97,65},{2,98}... | collective-permute-start | bytes 393224 | tf_op jit(solution)/shard_map/cond/branch_0_fun/ppermute | solution.py:366
  109.3 8.3 %all-to-all-done = bf16[16,208,256]{2,1,0:T(8,128)(2,1)} async-done(((bf16[16,208,256]{2,1,0:T(8,128)(2,1)}), bf16[16,208,256]{2,1,0:T(8,128)(2,1)}, u32[]{:S(2)}, u32[]{:S(2)}) %all-to-all-start) | async-done | bytes 1703968 | tf_op jit(solution)/shard_map/cond/branch_0_fun/all_to_all | solution.py:359
  119.9 2.3 %collective-permute-start.14 = (bf16[4,208,256]{2,1,0:T(8,128)(2,1)}, bf16[4,208,256]{2,1,0:T(8,128)(2,1)S(1)}, u32[]{:S(2)}, u32[]{:S(2)}) collective-permute-start(bf16[4,208,256]{2,1,0:T(8,128)(2,1)} %get-tuple-element.174.refs_0_), channel_id=1, source_target_pairs={{0,24},{8,0},{16,8},{24,16},{1,25},{9,1},{17,9},{25,17},{2,26},{10... | collective-permute-start | bytes 1277960 | tf_op jit(solution)/shard_map/ppermute | solution.py:380
  122.6 1.3 collective-permute-start.10
  124.5 6.4 %collective-permute-done.13.refs_1_ = bf16[4,208,256]{2,1,0:T(8,128)(2,1)S(1)} collective-permute-done((bf16[4,208,256]{2,1,0:T(8,128)(2,1)}, bf16[4,208,256]{2,1,0:T(8,128)(2,1)S(1)}, u32[]{:S(2)}, u32[]{:S(2)}) %collective-permute-start.13) | collective-permute-done | bytes 426016 | tf_op jit(solution)/shard_map/ppermute | solution.py:380
  130.9 2.3 %collective-permute-start.17 = (bf16[4,208,256]{2,1,0:T(8,128)(2,1)}, bf16[4,208,256]{2,1,0:T(8,128)(2,1)S(1)}, u32[]{:S(2)}, u32[]{:S(2)}) collective-permute-start(bf16[4,208,256]{2,1,0:T(8,128)(2,1)} %get-tuple-element.174.refs_0_), channel_id=1, source_target_pairs={{0,1},{1,0},{2,3},{3,2},{4,5},{5,4},{6,7},{7,6},{8,9},{9,8},{10,11... | collective-permute-start | bytes 1277960 | tf_op jit(solution)/shard_map/ppermute | solution.py:384
  133.3 2.7 %collective-permute-start.16 = (bf16[2,208,256]{2,1,0:T(8,128)(2,1)S(1)}, bf16[2,208,256]{2,1,0:T(8,128)(2,1)S(1)}, u32[]{:S(2)}, u32[]{:S(2)}) collective-permute-start(bf16[2,208,256]{2,1,0:T(8,128)(2,1)S(1)} %slice.119), channel_id=1, source_target_pairs={{0,24},{8,0},{16,8},{24,16},{1,25},{9,1},{17,9},{25,17},{2,26},{10... | collective-permute-start | bytes 638984 | tf_op jit(solution)/shard_map/ppermute | solution.py:382
  137.3 4.1 %collective-permute-done.15.refs_3_ = bf16[2,208,256]{2,1,0:T(8,128)(2,1)S(1)} collective-permute-done((bf16[2,208,256]{2,1,0:T(8,128)(2,1)S(1)}, bf16[2,208,256]{2,1,0:T(8,128)(2,1)S(1)}, u32[]{:S(2)}, u32[]{:S(2)}) %collective-permute-start.15) | collective-permute-done | bytes 213024 | tf_op jit(solution)/shard_map/ppermute | solution.py:382
  143.7 23.8 %attention.1 = bf16[4,128,512]{2,1,0:T(8,128)(2,1)S(1)} custom-call(s32[13]{0:T(128)S(1)} %pad_add_fusion.2.meta_ref, bf16[4,128,512]{2,1,0:T(8,128)(2,1)S(1)} %pad_maximum_fusion.3.q_ref, bf16[4,208,256]{2,1,0:T(8,128)(2,1)} %get-tuple-element.174.refs_0_, bf16[4,208,256]{2,1,0:T(8,128)(2,1)S(1)} %collective-permute-done.13.refs_1_, ...), custom_call_target="tpu_custom_call" | custom-call | flops 13958643712 | bytes 3407872 | tf_op jit(solution)/shard_map/attention/pallas_call | solution.py:220
  167.8 2.5 %collective-permute-start.22 = (bf16[128,512]{1,0:T(8,128)(2,1)S(1)}, bf16[128,512]{1,0:T(8,128)(2,1)S(1)}, u32[]{:S(2)}, u32[]{:S(2)}) collective-permute-start(bf16[128,512]{1,0:T(8,128)(2,1)S(1)} %get-tuple-element.226), channel_id=1, source_target_pairs={{0,6},{2,0},{4,2},{6,4},{1,7},{3,1},{5,3},{7,5},{8,14},{10,8},{12,... | collective-permute-start | bytes 393224 | tf_op jit(solution)/shard_map/ppermute | solution.py:396
  170.3 6.4 %collective-permute-done.24 = bf16[128,512]{1,0:T(8,128)(2,1)S(1)} collective-permute-done((bf16[128,512]{1,0:T(8,128)(2,1)S(1)}, bf16[128,512]{1,0:T(8,128)(2,1)S(1)}, u32[]{:S(2)}, u32[]{:S(2)}) %collective-permute-start.24) | collective-permute-done | bytes 131104 | tf_op jit(solution)/shard_map/ppermute | solution.py:396
  (98 shorter events, 19.9 us)
Async XLA Ops:
  6.5 68.3 %all-gather.2.cloned.1.call-start = ((), (), s32[]{:S(2)}) async-start(), calls=%async_computation.3 | async-start | bytes 12976128 | tf_op jit(solution)/shard_map/all_gather | solution.py:318
  9.4 20.7 %collective-permute-start.6 = (bf16[1601,4096]{1,0:T(8,128)(2,1)}, bf16[1601,4096]{1,0:T(8,128)(2,1)}, u32[]{:S(2)}, u32[]{:S(2)}) collective-permute-start(bf16[1601,4096]{1,0:T(8,128)(2,1)} %bitcast.70), channel_id=1, source_target_pairs={{0,1},{1,0},{2,3},{3,2},{4,5},{5,4},{6,7},{7,6},{8,9},{9,8},{10,11... | collective-permute-start | bytes 39346184 | tf_op jit(solution)/shard_map/ppermute | solution.py:319
  10.8 24.9 %collective-permute-start.7 = (bf16[128,4096]{1,0:T(8,128)(2,1)S(1)}, bf16[128,4096]{1,0:T(8,128)(2,1)S(1)}, u32[]{:S(2)}, u32[]{:S(2)}) collective-permute-start(bf16[128,4096]{1,0:T(8,128)(2,1)S(1)} %fusion.4), channel_id=1, source_target_pairs={{0,32},{32,64},{64,96},{96,0},{1,33},{33,65},{65,97},{97,1},{2,34}... | collective-permute-start | bytes 3145736 | tf_op jit(solution)/shard_map/ppermute | solution.py:323
  12.5 26.1 %collective-permute-start.8 = (bf16[128,4096]{1,0:T(8,128)(2,1)S(1)}, bf16[128,4096]{1,0:T(8,128)(2,1)}, u32[]{:S(2)}, u32[]{:S(2)}) collective-permute-start(bf16[128,4096]{1,0:T(8,128)(2,1)S(1)} %fusion.4), channel_id=1, source_target_pairs={{0,64},{32,96},{64,0},{96,32},{1,65},{33,97},{65,1},{97,33},{2,66}... | collective-permute-start | bytes 3145736 | tf_op jit(solution)/shard_map/ppermute | solution.py:323
  13.7 47.3 %collective-permute-start.9 = (bf16[128,4096]{1,0:T(8,128)(2,1)S(1)}, bf16[128,4096]{1,0:T(8,128)(2,1)}, u32[]{:S(2)}, u32[]{:S(2)}) collective-permute-start(bf16[128,4096]{1,0:T(8,128)(2,1)S(1)} %fusion.4), channel_id=1, source_target_pairs={{0,96},{32,0},{64,32},{96,64},{1,97},{33,1},{65,33},{97,65},{2,98}... | collective-permute-start | bytes 3145736 | tf_op jit(solution)/shard_map/ppermute | solution.py:323
  86.2 31.5 %all-to-all-start = ((bf16[16,208,256]{2,1,0:T(8,128)(2,1)}), bf16[16,208,256]{2,1,0:T(8,128)(2,1)}, u32[]{:S(2)}, u32[]{:S(2)}) async-start(bf16[16,208,256]{2,1,0:T(8,128)(2,1)} %get-tuple-element.113), calls=%async_computation | async-start | bytes 3407872 | tf_op jit(solution)/shard_map/cond/branch_0_fun/all_to_all | solution.py:359
  97.0 12.2 %collective-permute-start.2 = (bf16[128,512]{1,0:T(8,128)(2,1)S(1)}, bf16[128,512]{1,0:T(8,128)(2,1)S(1)}, u32[]{:S(2)}, u32[]{:S(2)}) collective-permute-start(bf16[128,512]{1,0:T(8,128)(2,1)S(1)} %get-tuple-element.196), channel_id=1, source_target_pairs={{0,32},{32,64},{64,96},{96,0},{1,33},{33,65},{65,97},{97,1},{2,34}... | collective-permute-start | bytes 393224 | tf_op jit(solution)/shard_map/cond/branch_0_fun/ppermute | solution.py:366
  98.3 10.9 %collective-permute-start.1 = (bf16[128,512]{1,0:T(8,128)(2,1)S(1)}, bf16[128,512]{1,0:T(8,128)(2,1)S(1)}, u32[]{:S(2)}, u32[]{:S(2)}) collective-permute-start(bf16[128,512]{1,0:T(8,128)(2,1)S(1)} %get-tuple-element.197), channel_id=1, source_target_pairs={{0,64},{32,96},{64,0},{96,32},{1,65},{33,97},{65,1},{97,33},{2,66}... | collective-permute-start | bytes 393224 | tf_op jit(solution)/shard_map/cond/branch_0_fun/ppermute | solution.py:366
  99.1 10.1 %collective-permute-start = (bf16[128,512]{1,0:T(8,128)(2,1)S(1)}, bf16[128,512]{1,0:T(8,128)(2,1)S(1)}, u32[]{:S(2)}, u32[]{:S(2)}) collective-permute-start(bf16[128,512]{1,0:T(8,128)(2,1)S(1)} %get-tuple-element.198), channel_id=1, source_target_pairs={{0,96},{32,0},{64,32},{96,64},{1,97},{33,1},{65,33},{97,65},{2,98}... | collective-permute-start | bytes 393224 | tf_op jit(solution)/shard_map/cond/branch_0_fun/ppermute | solution.py:366
  119.5 11.4 %collective-permute-start.13 = (bf16[4,208,256]{2,1,0:T(8,128)(2,1)}, bf16[4,208,256]{2,1,0:T(8,128)(2,1)S(1)}, u32[]{:S(2)}, u32[]{:S(2)}) collective-permute-start(bf16[4,208,256]{2,1,0:T(8,128)(2,1)} %get-tuple-element.174.refs_0_), channel_id=1, source_target_pairs={{0,8},{8,16},{16,24},{24,0},{1,9},{9,17},{17,25},{25,1},{2,10},{10... | collective-permute-start | bytes 1277960 | tf_op jit(solution)/shard_map/ppermute | solution.py:380
  119.9 13.3 %collective-permute-start.14 = (bf16[4,208,256]{2,1,0:T(8,128)(2,1)}, bf16[4,208,256]{2,1,0:T(8,128)(2,1)S(1)}, u32[]{:S(2)}, u32[]{:S(2)}) collective-permute-start(bf16[4,208,256]{2,1,0:T(8,128)(2,1)} %get-tuple-element.174.refs_0_), channel_id=1, source_target_pairs={{0,24},{8,0},{16,8},{24,16},{1,25},{9,1},{17,9},{25,17},{2,26},{10... | collective-permute-start | bytes 1277960 | tf_op jit(solution)/shard_map/ppermute | solution.py:380
  122.4 11.0 %collective-permute-start.12 = (bf16[128,512]{1,0:T(8,128)(2,1)S(1)}, bf16[128,512]{1,0:T(8,128)(2,1)S(1)}, u32[]{:S(2)}, u32[]{:S(2)}) collective-permute-start(bf16[128,512]{1,0:T(8,128)(2,1)S(1)} %get-tuple-element.228), channel_id=1, source_target_pairs={{0,6},{2,0},{4,2},{6,4},{1,7},{3,1},{5,3},{7,5},{8,14},{10,8},{12,... | collective-permute-start | bytes 393224 | tf_op jit(solution)/shard_map/ppermute | solution.py:386
  122.4 13.6 %collective-permute-start.11 = (bf16[128,512]{1,0:T(8,128)(2,1)S(1)}, bf16[128,512]{1,0:T(8,128)(2,1)S(1)}, u32[]{:S(2)}, u32[]{:S(2)}) collective-permute-start(bf16[128,512]{1,0:T(8,128)(2,1)S(1)} %get-tuple-element.229), channel_id=1, source_target_pairs={{0,4},{2,6},{4,0},{6,2},{1,5},{3,7},{5,1},{7,3},{8,12},{10,14},{12... | collective-permute-start | bytes 393224 | tf_op jit(solution)/shard_map/ppermute | solution.py:386
  122.6 14.1 %collective-permute-start.10 = (bf16[128,512]{1,0:T(8,128)(2,1)S(1)}, bf16[128,512]{1,0:T(8,128)(2,1)S(1)}, u32[]{:S(2)}, u32[]{:S(2)}) collective-permute-start(bf16[128,512]{1,0:T(8,128)(2,1)S(1)} %get-tuple-element.230), channel_id=1, source_target_pairs={{0,2},{2,4},{4,6},{6,0},{1,3},{3,5},{5,7},{7,1},{8,10},{10,12},{12... | collective-permute-start | bytes 393224 | tf_op jit(solution)/shard_map/ppermute | solution.py:386
  130.9 11.4 %collective-permute-start.17 = (bf16[4,208,256]{2,1,0:T(8,128)(2,1)}, bf16[4,208,256]{2,1,0:T(8,128)(2,1)S(1)}, u32[]{:S(2)}, u32[]{:S(2)}) collective-permute-start(bf16[4,208,256]{2,1,0:T(8,128)(2,1)} %get-tuple-element.174.refs_0_), channel_id=1, source_target_pairs={{0,1},{1,0},{2,3},{3,2},{4,5},{5,4},{6,7},{7,6},{8,9},{9,8},{10,11... | collective-permute-start | bytes 1277960 | tf_op jit(solution)/shard_map/ppermute | solution.py:384
  133.2 8.2 %collective-permute-start.15 = (bf16[2,208,256]{2,1,0:T(8,128)(2,1)S(1)}, bf16[2,208,256]{2,1,0:T(8,128)(2,1)S(1)}, u32[]{:S(2)}, u32[]{:S(2)}) collective-permute-start(bf16[2,208,256]{2,1,0:T(8,128)(2,1)S(1)} %slice.118), channel_id=1, source_target_pairs={{0,8},{8,16},{16,24},{24,0},{1,9},{9,17},{17,25},{25,1},{2,10},{10... | collective-permute-start | bytes 638984 | tf_op jit(solution)/shard_map/ppermute | solution.py:382
  133.3 8.8 %collective-permute-start.16 = (bf16[2,208,256]{2,1,0:T(8,128)(2,1)S(1)}, bf16[2,208,256]{2,1,0:T(8,128)(2,1)S(1)}, u32[]{:S(2)}, u32[]{:S(2)}) collective-permute-start(bf16[2,208,256]{2,1,0:T(8,128)(2,1)S(1)} %slice.119), channel_id=1, source_target_pairs={{0,24},{8,0},{16,8},{24,16},{1,25},{9,1},{17,9},{25,17},{2,26},{10... | collective-permute-start | bytes 638984 | tf_op jit(solution)/shard_map/ppermute | solution.py:382
  136.1 6.3 %collective-permute-start.18 = (bf16[4,208,256]{2,1,0:T(8,128)(2,1)S(1)}, bf16[4,208,256]{2,1,0:T(8,128)(2,1)S(1)}, u32[]{:S(2)}, u32[]{:S(2)}) collective-permute-start(bf16[4,208,256]{2,1,0:T(8,128)(2,1)S(1)} %collective-permute-done.13.refs_1_), channel_id=1, source_target_pairs={{0,1},{1,0},{2,3},{3,2},{4,5},{5,4},{6,7},{7,6},{8,9},{9,8},{10,11... | collective-permute-start | bytes 1277960 | tf_op jit(solution)/shard_map/ppermute | solution.py:384
  136.6 5.7 %collective-permute-start.19 = (bf16[4,208,256]{2,1,0:T(8,128)(2,1)S(1)}, bf16[4,208,256]{2,1,0:T(8,128)(2,1)S(1)}, u32[]{:S(2)}, u32[]{:S(2)}) collective-permute-start(bf16[4,208,256]{2,1,0:T(8,128)(2,1)S(1)} %collective-permute-done.14.refs_2_), channel_id=1, source_target_pairs={{0,1},{1,0},{2,3},{3,2},{4,5},{5,4},{6,7},{7,6},{8,9},{9,8},{10,11... | collective-permute-start | bytes 1277960 | tf_op jit(solution)/shard_map/ppermute | solution.py:384
  141.4 1.9 %collective-permute-start.20 = (bf16[2,208,256]{2,1,0:T(8,128)(2,1)S(1)}, bf16[2,208,256]{2,1,0:T(8,128)(2,1)S(1)}, u32[]{:S(2)}, u32[]{:S(2)}) collective-permute-start(bf16[2,208,256]{2,1,0:T(8,128)(2,1)S(1)} %collective-permute-done.15.refs_3_), channel_id=1, source_target_pairs={{0,1},{1,0},{2,3},{3,2},{4,5},{5,4},{6,7},{7,6},{8,9},{9,8},{10,11... | collective-permute-start | bytes 638984 | tf_op jit(solution)/shard_map/ppermute | solution.py:384
  142.2 1.5 collective-permute-start.21
  167.5 9.2 %collective-permute-start.24 = (bf16[128,512]{1,0:T(8,128)(2,1)S(1)}, bf16[128,512]{1,0:T(8,128)(2,1)S(1)}, u32[]{:S(2)}, u32[]{:S(2)}) collective-permute-start(bf16[128,512]{1,0:T(8,128)(2,1)S(1)} %get-tuple-element.224), channel_id=1, source_target_pairs={{0,2},{2,4},{4,6},{6,0},{1,3},{3,5},{5,7},{7,1},{8,10},{10,12},{12... | collective-permute-start | bytes 393224 | tf_op jit(solution)/shard_map/ppermute | solution.py:396
  167.6 9.1 %collective-permute-start.23 = (bf16[128,512]{1,0:T(8,128)(2,1)S(1)}, bf16[128,512]{1,0:T(8,128)(2,1)S(1)}, u32[]{:S(2)}, u32[]{:S(2)}) collective-permute-start(bf16[128,512]{1,0:T(8,128)(2,1)S(1)} %get-tuple-element.225), channel_id=1, source_target_pairs={{0,4},{2,6},{4,0},{6,2},{1,5},{3,7},{5,1},{7,3},{8,12},{10,14},{12... | collective-permute-start | bytes 393224 | tf_op jit(solution)/shard_map/ppermute | solution.py:396
  167.8 9.0 %collective-permute-start.22 = (bf16[128,512]{1,0:T(8,128)(2,1)S(1)}, bf16[128,512]{1,0:T(8,128)(2,1)S(1)}, u32[]{:S(2)}, u32[]{:S(2)}) collective-permute-start(bf16[128,512]{1,0:T(8,128)(2,1)S(1)} %get-tuple-element.226), channel_id=1, source_target_pairs={{0,6},{2,0},{4,2},{6,4},{1,7},{3,1},{5,3},{7,5},{8,14},{10,8},{12,... | collective-permute-start | bytes 393224 | tf_op jit(solution)/shard_map/ppermute | solution.py:396
  (10 other events, 157.8 us)
Sparse Core Ops, SparseCore 0:
  9.6 65.2 all-gather.1
where the time goes:
time: 185 us
  waiting for transfers between devices  76.6 us (41%)
  Pallas kernels  40.9 us (22%)
  starting transfers between devices  28.1 us (15%)
  between operations  16.2 us (9%)
  other arithmetic  8.98 us (5%)
  loops' own time  7.52 us (4%)
  local copies, waits for them, and re-layouts  6.28 us (3%)
    ppermute x3, waiting for transfers between devices, local(): lax.ppermute(normed, 'z', ring(step))  30 us
    pallas_call x1, Pallas kernels, attend(): pl.pallas_call(functools.partial(attend_kernel, pad), grid_spec=pltpu.Pre...  23.8 us
    all_gather x1, waiting for transfers between devices, local(): lax.all_gather(jnp.concatenate([k_weight, v_weight, q_share], axis=1), SE...  13.9 us
    pallas_call x1, Pallas kernels, project_kv(): pl.pallas_call(functools.partial(kv_kernel, tile_len), in_specs=[pl.Block...  11.3 us
    all_to_all x1, waiting for transfers between devices, send(): return lax.all_to_all(sent, PLANE, 0, 0, tiled=True)  8.35 us
    another operation x1, loops' own time, local(): chosen, mine = lax.cond(crowded, spread_two, spread_one)  7.52 us
    ppermute x3, waiting for transfers between devices, local(): lax.ppermute(context[k], 'x', ring(-k))  6.48 us
    ppermute x1, waiting for transfers between devices, local(): lax.ppermute(chosen, 'y', after)  6.44 us
  transfers between devices with their start and end apart: 24, of which 12 were waited for; matrix products, arithmetic and copies ran while one was open for 5% of the time, Pallas kernels for 3%

commit v1 on v0

--- a/solution.py
+++ b/solution.py
@@ -155,36 +155,40 @@
         acc_ref[...] = jnp.zeros_like(acc_ref)
 
     low, high = meta_ref[tile], meta_ref[4 + tile]
-    some, every = False, True
+    some = False
     for b in range(blocks):
         first = meta_ref[8 + b]
         some = some | ((low < first + rows) & (high > first))
-        every = every & (low <= first) & (high >= first + rows)
-
-    def step(partial):
+
+    @pl.when(some)
+    def _():
         held = []
         for own, before, after, low_tiles, high_tiles in (part_refs[:5], part_refs[5:]):
-            opposite = jnp.where(tile < 2, low_tiles[0], high_tiles[0])
-            held += [own[0], before[0], after[0], opposite]
+            held += [own[0], before[0], after[0], jnp.where(tile < 2, low_tiles[0], high_tiles[0])]
         kv = jnp.concatenate(held, axis=0)
         row = lax.broadcasted_iota(jnp.int32, (keys, 128), 0)
+        lane = lax.broadcasted_iota(jnp.int32, (keys, 128), 1)
         padding = (row >= meta_ref[8 + blocks]) & (row < meta_ref[8 + blocks] + pad)
-        lane = lax.broadcasted_iota(jnp.int32, (keys, 128), 1) == 0
-        bias = jnp.where(padding & lane, MASKED, 0.0).astype(jnp.bfloat16)
-        key = jnp.concatenate([kv[:, :128], bias], axis=1)
+        key_mask = jnp.where((lane == 0) & padding, MASKED, jnp.where(lane == 1, 1.0, 0.0))
+        key = jnp.concatenate([kv[:, :128], key_mask.astype(jnp.bfloat16)], axis=1)
         value = jnp.concatenate([kv[:, 128:], jnp.ones((keys, 128), jnp.bfloat16)], axis=1)
-        one = (lax.broadcasted_iota(jnp.int32, (2 * rows, 128), 1) == 0).astype(jnp.bfloat16)
+        text_row = lax.broadcasted_iota(jnp.int32, (rows, 128), 0)
+        text_lane = lax.broadcasted_iota(jnp.int32, (rows, 128), 1)
 
         def score(group):
             b, h = group // pairs, group % pairs * 2
-            both = [q_ref[b, :, i * 128 : (i + 1) * 128] for i in (h, h + 1)]
-            deep = jnp.concatenate([jnp.concatenate(both, axis=0), one], axis=1)
-            return lax.dot_general(deep, key, (((1,), (1,)), ((), ())), preferred_element_type=jnp.float32)
+            at = meta_ref[8 + b] + text_row
+            outside = (at < low) | (at >= high)
+            mask = jnp.where((text_lane == 1) & outside, MASKED, jnp.where(text_lane == 0, 1.0, 0.0))
+            mask = mask.astype(jnp.bfloat16)
+            both = [
+                jnp.concatenate([q_ref[b, :, i * 128 : (i + 1) * 128], mask], axis=1) for i in (h, h + 1)
+            ]
+            return lax.dot_general(
+                jnp.concatenate(both, axis=0), key, (((1,), (1,)), ((), ())), preferred_element_type=jnp.float32
+            )
 
         def soften(group, scores):
-            if partial:
-                at = meta_ref[8 + group // pairs] + lax.broadcasted_iota(jnp.int32, (2 * rows, 1), 0) % rows
-                scores = jnp.where((at >= low) & (at < high), scores, MASKED)
             m_old = m_ref[group]
             m_new = jnp.maximum(m_old, jnp.max(scores, axis=1, keepdims=True))
             probs = jnp.exp2((scores - m_new) * factor)
@@ -199,9 +203,6 @@
             ahead = score(group + 1) if group + 1 < blocks * pairs else None
             soften(group, scores)
             scores = ahead
-
-    pl.when(every)(lambda: step(False))
-    pl.when(some & jnp.logical_not(every))(lambda: step(True))
 
     @pl.when(tile == pl.num_programs(0) - 1)
     def _():
@@ -376,12 +377,11 @@
 
     chosen, mine = lax.cond(crowded, spread_two, spread_one)
 
-    after, before, swap = ring(1), ring(-1), [(0, 1), (1, 0)]
-    from_before, from_after = lax.ppermute(chosen, "y", after), lax.ppermute(chosen, "y", before)
+    before, after = lax.ppermute(chosen, "y", ring(1)), lax.ppermute(chosen, "y", ring(-1))
     half = most_tiles // 2
-    opposite = [lax.ppermute(from_before[:half], "y", after), lax.ppermute(from_after[half:], "y", before)]
-    parts = [chosen, from_before, from_after, *opposite]
-    parts += [lax.ppermute(part, "c", swap) for part in parts]
+    opposite = [lax.ppermute(before[:half], "y", ring(1)), lax.ppermute(after[half:], "y", ring(-1))]
+    parts = [chosen, before, after, *opposite]
+    parts += [lax.ppermute(part, "c", [(0, 1), (1, 0)]) for part in parts]
     query = [mine[(at_x + s - at_doc) % 4] for s in range(4)]
     query = [query[0]] + [lax.ppermute(query[s], "x", ring(s)) for s in (1, 2, 3)]
     last_slot = jnp.array([1, 3, 2, 0], jnp.int32)[at_y]

time: 185 us -> 184 us (level)
  the two profiles are of different devices: /device:TPU:33 before, /device:TPU:80 now
where the time goes in v1:
time: 184 us; the launch traced here: 181 us
  waiting for transfers between devices  79.2 us (43%)
  Pallas kernels  39.1 us (21%)
  starting transfers between devices  23.7 us (13%)
  between operations  16.3 us (9%)
  other arithmetic  8.98 us (5%)
  loops' own time  7.52 us (4%)
  local copies, waits for them, and re-layouts  6.28 us (3%)
    ppermute x3, waiting for transfers between devices, local(): lax.ppermute(normed, 'z', ring(step))  29.5 us
    pallas_call x1, Pallas kernels, attend(): pl.pallas_call(functools.partial(attend_kernel, pad), grid_spec=pltpu.Pre...  22 us
    all_gather x1, waiting for transfers between devices, local(): lax.all_gather(jnp.concatenate([k_weight, v_weight, q_share], axis=1), SE...  13.4 us
    pallas_call x1, Pallas kernels, project_kv(): pl.pallas_call(functools.partial(kv_kernel, tile_len), in_specs=[pl.Block...  11.3 us
    ppermute x1, waiting for transfers between devices, local(): other_rows = lax.ppermute(tile_rows, 'c', [(0, 1), (1, 0)])  8.01 us
    all_to_all x1, waiting for transfers between devices, send(): return lax.all_to_all(sent, PLANE, 0, 0, tiled=True)  7.63 us
    another operation x1, loops' own time, local(): chosen, mine = lax.cond(crowded, spread_two, spread_one)  7.52 us
    ppermute x3, waiting for transfers between devices, local(): lax.ppermute(context[k], 'x', ring(-k))  6.94 us
  transfers between devices with their start and end apart: 24, of which 12 were waited for; matrix products, arithmetic and copies ran while one was open for 5% of the time, Pallas kernels for 3%

profile of v1, /device:TPU:80, one launch (start us, length us, event | category | flops | bytes accessed | tf_op | source)
XLA Modules:
  0.0 181.1 jit_solution(10014820177995256295)
XLA Ops:
  7.6 1.8 pad_maximum_fusion.6
  10.2 1.7 collective-permute-start.7
  11.9 1.6 collective-permute-start.9
  21.8 8.0 %collective-permute-done.6.other_ref = bf16[1601,4096]{1,0:T(8,128)(2,1)} collective-permute-done((bf16[1601,4096]{1,0:T(8,128)(2,1)}, bf16[1601,4096]{1,0:T(8,128)(2,1)}, u32[]{:S(2)}, u32[]{:S(2)}) %collective-permute-start.6) | collective-permute-done | bytes 13115424 | tf_op jit(solution)/shard_map/ppermute | solution.py:320
  30.7 27.5 %collective-permute-done.7 = bf16[128,4096]{1,0:T(8,128)(2,1)S(1)} collective-permute-done((bf16[128,4096]{1,0:T(8,128)(2,1)S(1)}, bf16[128,4096]{1,0:T(8,128)(2,1)S(1)}, u32[]{:S(2)}, u32[]{:S(2)}) %collective-permute-start.7) | collective-permute-done | bytes 1048608 | tf_op jit(solution)/shard_map/ppermute | solution.py:324
  58.3 1.9 %collective-permute-done.9 = bf16[128,4096]{1,0:T(8,128)(2,1)} collective-permute-done((bf16[128,4096]{1,0:T(8,128)(2,1)S(1)}, bf16[128,4096]{1,0:T(8,128)(2,1)}, u32[]{:S(2)}, u32[]{:S(2)}) %collective-permute-start.9) | collective-permute-done | bytes 1048608 | tf_op jit(solution)/shard_map/ppermute | solution.py:324
  60.2 13.4 %all-gather.2.cloned.1.call-done.weight_ref = bf16[4096,1536]{1,0:T(8,128)(2,1)} async-done(((bf16[128,1536]{1,0:T(8,128)(2,1)}), bf16[4096,1536]{1,0:T(8,128)(2,1)}) %all-gather.2.cloned.1.call-update) | async-done | bytes 12582928 | tf_op jit(solution)/shard_map/all_gather | solution.py:319
  73.6 11.3 %kv_projection.3 = bf16[16,208,256]{2,1,0:T(8,128)(2,1)} custom-call(s32[2]{0:T(128)S(1)} %pad_add_fusion.3.meta_ref, bf16[1601,4096]{1,0:T(8,128)(2,1)} %bitcast.71, bf16[1601,4096]{1,0:T(8,128)(2,1)} %collective-permute-done.6.other_ref, bf16[16,4096]{1,0:T(8,128)(2,1)S(1)} %pad.7.own_tail, bf16[16,4096]{1,0:T(8,128)(2,1)S(1)} %pad.8.other_tail, ...), custom_call_target="tpu_custom_call" | custom-call | flops 6979321856 | bytes 15204352 | tf_op jit(solution)/shard_map/kv_projection/pallas_call | solution.py:119
  84.9 32.6 %conditional.1 = (bf16[4,208,256]{2,1,0:T(8,128)(2,1)}, bf16[4,128,512]{2,1,0:T(8,128)(2,1)S(1)}) conditional(s32[]{:T(128)} %convert_element_type.21, (bf16[16,208,256]{2,1,0:T(8,128)(2,1)}, f32[128]{0:T(128)S(1)}, bf16[128,4096]{1,0:T(8,128)(2,1)S(1)}, bf16[128,4096]{1,0:T(8,128)(2,1)S(1)}, bf16[128,4096]{1,0:T(8,128)(2,1)}, ...), branch_computations={%region_14.15_spmd, %region_15.16_spmd} | conditional | flops 9129083904 | bytes 40473188 | solution.py:378
  84.9 5.9 %all-to-all-start = ((bf16[16,208,256]{2,1,0:T(8,128)(2,1)}), bf16[16,208,256]{2,1,0:T(8,128)(2,1)}, u32[]{:S(2)}, u32[]{:S(2)}) async-start(bf16[16,208,256]{2,1,0:T(8,128)(2,1)} %get-tuple-element.113), calls=%async_computation | async-start | bytes 3407872 | tf_op jit(solution)/shard_map/cond/branch_0_fun/all_to_all | solution.py:360
  90.8 5.8 %query_projection.2 = bf16[4,128,512]{2,1,0:T(8,128)(2,1)S(1)} custom-call(bf16[128,4096]{1,0:T(8,128)(2,1)S(1)} %get-tuple-element.114.text0, bf16[128,4096]{1,0:T(8,128)(2,1)S(1)} %get-tuple-element.115.text1, bf16[128,4096]{1,0:T(8,128)(2,1)} %get-tuple-element.116.text2, bf16[128,4096]{1,0:T(8,128)(2,1)} %get-tuple-element.117.text3, ...), custom_call_target="tpu_custom_call" | custom-call | flops 2147483648 | bytes 8388608 | tf_op jit(solution)/shard_map/cond/branch_0_fun/query_projection/pallas_call | solution.py:279
  96.7 1.3 collective-permute-start.2
  108.0 7.6 %all-to-all-done = bf16[16,208,256]{2,1,0:T(8,128)(2,1)} async-done(((bf16[16,208,256]{2,1,0:T(8,128)(2,1)}), bf16[16,208,256]{2,1,0:T(8,128)(2,1)}, u32[]{:S(2)}, u32[]{:S(2)}) %all-to-all-start) | async-done | bytes 1703968 | tf_op jit(solution)/shard_map/cond/branch_0_fun/all_to_all | solution.py:360
  117.5 2.4 %collective-permute-start.13 = (bf16[4,208,256]{2,1,0:T(8,128)(2,1)}, bf16[4,208,256]{2,1,0:T(8,128)(2,1)S(1)}, u32[]{:S(2)}, u32[]{:S(2)}) collective-permute-start(bf16[4,208,256]{2,1,0:T(8,128)(2,1)} %get-tuple-element.174.refs_0_), channel_id=1, source_target_pairs={{0,8},{8,16},{16,24},{24,0},{1,9},{9,17},{17,25},{25,1},{2,10},{10... | collective-permute-start | bytes 1277960 | tf_op jit(solution)/shard_map/ppermute | solution.py:380
  121.1 1.3 collective-permute-start.10
  123.1 5.6 %collective-permute-done.13.refs_1_ = bf16[4,208,256]{2,1,0:T(8,128)(2,1)S(1)} collective-permute-done((bf16[4,208,256]{2,1,0:T(8,128)(2,1)}, bf16[4,208,256]{2,1,0:T(8,128)(2,1)S(1)}, u32[]{:S(2)}, u32[]{:S(2)}) %collective-permute-start.13) | collective-permute-done | bytes 426016 | tf_op jit(solution)/shard_map/ppermute | solution.py:380
  128.7 2.0 %collective-permute-done.14.refs_2_ = bf16[4,208,256]{2,1,0:T(8,128)(2,1)S(1)} collective-permute-done((bf16[4,208,256]{2,1,0:T(8,128)(2,1)}, bf16[4,208,256]{2,1,0:T(8,128)(2,1)S(1)}, u32[]{:S(2)}, u32[]{:S(2)}) %collective-permute-start.14) | collective-permute-done | bytes 426016 | tf_op jit(solution)/shard_map/ppermute | solution.py:380
  130.7 2.7 %collective-permute-start.15 = (bf16[2,208,256]{2,1,0:T(8,128)(2,1)S(1)}, bf16[2,208,256]{2,1,0:T(8,128)(2,1)S(1)}, u32[]{:S(2)}, u32[]{:S(2)}) collective-permute-start(bf16[2,208,256]{2,1,0:T(8,128)(2,1)S(1)} %slice.118), channel_id=1, source_target_pairs={{0,8},{8,16},{16,24},{24,0},{1,9},{9,17},{17,25},{25,1},{2,10},{10... | collective-permute-start | bytes 638984 | tf_op jit(solution)/shard_map/ppermute | solution.py:382
  134.7 2.1 %collective-permute-done.15.refs_3_ = bf16[2,208,256]{2,1,0:T(8,128)(2,1)S(1)} collective-permute-done((bf16[2,208,256]{2,1,0:T(8,128)(2,1)S(1)}, bf16[2,208,256]{2,1,0:T(8,128)(2,1)S(1)}, u32[]{:S(2)}, u32[]{:S(2)}) %collective-permute-start.15) | collective-permute-done | bytes 213024 | tf_op jit(solution)/shard_map/ppermute | solution.py:382
  136.7 2.8 %collective-permute-done.16.refs_4_ = bf16[2,208,256]{2,1,0:T(8,128)(2,1)S(1)} collective-permute-done((bf16[2,208,256]{2,1,0:T(8,128)(2,1)S(1)}, bf16[2,208,256]{2,1,0:T(8,128)(2,1)S(1)}, u32[]{:S(2)}, u32[]{:S(2)}) %collective-permute-start.16) | collective-permute-done | bytes 213024 | tf_op jit(solution)/shard_map/ppermute | solution.py:382
  139.7 1.3 collective-permute-done.21.refs_9_
  141.0 22.0 %attention.1 = bf16[4,128,512]{2,1,0:T(8,128)(2,1)S(1)} custom-call(s32[13]{0:T(128)S(1)} %pad_add_fusion.2.meta_ref, bf16[4,128,512]{2,1,0:T(8,128)(2,1)S(1)} %pad_maximum_fusion.3.q_ref, bf16[4,208,256]{2,1,0:T(8,128)(2,1)} %get-tuple-element.174.refs_0_, bf16[4,208,256]{2,1,0:T(8,128)(2,1)S(1)} %collective-permute-done.13.refs_1_, ...), custom_call_target="tpu_custom_call" | custom-call | flops 13958643712 | bytes 3407872 | tf_op jit(solution)/shard_map/attention/pallas_call | solution.py:221
  163.7 2.6 %collective-permute-start.22 = (bf16[128,512]{1,0:T(8,128)(2,1)S(1)}, bf16[128,512]{1,0:T(8,128)(2,1)S(1)}, u32[]{:S(2)}, u32[]{:S(2)}) collective-permute-start(bf16[128,512]{1,0:T(8,128)(2,1)S(1)} %get-tuple-element.226), channel_id=1, source_target_pairs={{0,6},{2,0},{4,2},{6,4},{1,7},{3,1},{5,3},{7,5},{8,14},{10,8},{12,... | collective-permute-start | bytes 393224 | tf_op jit(solution)/shard_map/ppermute | solution.py:396
  166.3 6.3 %collective-permute-done.24 = bf16[128,512]{1,0:T(8,128)(2,1)S(1)} collective-permute-done((bf16[128,512]{1,0:T(8,128)(2,1)S(1)}, bf16[128,512]{1,0:T(8,128)(2,1)S(1)}, u32[]{:S(2)}, u32[]{:S(2)}) %collective-permute-start.24) | collective-permute-done | bytes 131104 | tf_op jit(solution)/shard_map/ppermute | solution.py:396
  (98 shorter events, 18.4 us)
Async XLA Ops:
  6.5 67.0 %all-gather.2.cloned.1.call-start = ((), (), s32[]{:S(2)}) async-start(), calls=%async_computation.3 | async-start | bytes 12976128 | tf_op jit(solution)/shard_map/all_gather | solution.py:319
  9.4 20.4 %collective-permute-start.6 = (bf16[1601,4096]{1,0:T(8,128)(2,1)}, bf16[1601,4096]{1,0:T(8,128)(2,1)}, u32[]{:S(2)}, u32[]{:S(2)}) collective-permute-start(bf16[1601,4096]{1,0:T(8,128)(2,1)} %bitcast.70), channel_id=1, source_target_pairs={{0,1},{1,0},{2,3},{3,2},{4,5},{5,4},{6,7},{7,6},{8,9},{9,8},{10,11... | collective-permute-start | bytes 39346184 | tf_op jit(solution)/shard_map/ppermute | solution.py:320
  10.2 48.1 %collective-permute-start.7 = (bf16[128,4096]{1,0:T(8,128)(2,1)S(1)}, bf16[128,4096]{1,0:T(8,128)(2,1)S(1)}, u32[]{:S(2)}, u32[]{:S(2)}) collective-permute-start(bf16[128,4096]{1,0:T(8,128)(2,1)S(1)} %fusion.4), channel_id=1, source_target_pairs={{0,32},{32,64},{64,96},{96,0},{1,33},{33,65},{65,97},{97,1},{2,34}... | collective-permute-start | bytes 3145736 | tf_op jit(solution)/shard_map/ppermute | solution.py:324
  11.9 46.4 %collective-permute-start.8 = (bf16[128,4096]{1,0:T(8,128)(2,1)S(1)}, bf16[128,4096]{1,0:T(8,128)(2,1)}, u32[]{:S(2)}, u32[]{:S(2)}) collective-permute-start(bf16[128,4096]{1,0:T(8,128)(2,1)S(1)} %fusion.4), channel_id=1, source_target_pairs={{0,64},{32,96},{64,0},{96,32},{1,65},{33,97},{65,1},{97,33},{2,66}... | collective-permute-start | bytes 3145736 | tf_op jit(solution)/shard_map/ppermute | solution.py:324
  11.9 48.3 %collective-permute-start.9 = (bf16[128,4096]{1,0:T(8,128)(2,1)S(1)}, bf16[128,4096]{1,0:T(8,128)(2,1)}, u32[]{:S(2)}, u32[]{:S(2)}) collective-permute-start(bf16[128,4096]{1,0:T(8,128)(2,1)S(1)} %fusion.4), channel_id=1, source_target_pairs={{0,96},{32,0},{64,32},{96,64},{1,97},{33,1},{65,33},{97,65},{2,98}... | collective-permute-start | bytes 3145736 | tf_op jit(solution)/shard_map/ppermute | solution.py:324
  84.9 30.7 %all-to-all-start = ((bf16[16,208,256]{2,1,0:T(8,128)(2,1)}), bf16[16,208,256]{2,1,0:T(8,128)(2,1)}, u32[]{:S(2)}, u32[]{:S(2)}) async-start(bf16[16,208,256]{2,1,0:T(8,128)(2,1)} %get-tuple-element.113), calls=%async_computation | async-start | bytes 3407872 | tf_op jit(solution)/shard_map/cond/branch_0_fun/all_to_all | solution.py:360
  96.7 11.2 %collective-permute-start.2 = (bf16[128,512]{1,0:T(8,128)(2,1)S(1)}, bf16[128,512]{1,0:T(8,128)(2,1)S(1)}, u32[]{:S(2)}, u32[]{:S(2)}) collective-permute-start(bf16[128,512]{1,0:T(8,128)(2,1)S(1)} %get-tuple-element.196), channel_id=1, source_target_pairs={{0,32},{32,64},{64,96},{96,0},{1,33},{33,65},{65,97},{97,1},{2,34}... | collective-permute-start | bytes 393224 | tf_op jit(solution)/shard_map/cond/branch_0_fun/ppermute | solution.py:367
  98.0 9.9 %collective-permute-start.1 = (bf16[128,512]{1,0:T(8,128)(2,1)S(1)}, bf16[128,512]{1,0:T(8,128)(2,1)S(1)}, u32[]{:S(2)}, u32[]{:S(2)}) collective-permute-start(bf16[128,512]{1,0:T(8,128)(2,1)S(1)} %get-tuple-element.197), channel_id=1, source_target_pairs={{0,64},{32,96},{64,0},{96,32},{1,65},{33,97},{65,1},{97,33},{2,66}... | collective-permute-start | bytes 393224 | tf_op jit(solution)/shard_map/cond/branch_0_fun/ppermute | solution.py:367
  98.7 9.2 %collective-permute-start = (bf16[128,512]{1,0:T(8,128)(2,1)S(1)}, bf16[128,512]{1,0:T(8,128)(2,1)S(1)}, u32[]{:S(2)}, u32[]{:S(2)}) collective-permute-start(bf16[128,512]{1,0:T(8,128)(2,1)S(1)} %get-tuple-element.198), channel_id=1, source_target_pairs={{0,96},{32,0},{64,32},{96,64},{1,97},{33,1},{65,33},{97,65},{2,98}... | collective-permute-start | bytes 393224 | tf_op jit(solution)/shard_map/cond/branch_0_fun/ppermute | solution.py:367
  117.5 11.2 %collective-permute-start.13 = (bf16[4,208,256]{2,1,0:T(8,128)(2,1)}, bf16[4,208,256]{2,1,0:T(8,128)(2,1)S(1)}, u32[]{:S(2)}, u32[]{:S(2)}) collective-permute-start(bf16[4,208,256]{2,1,0:T(8,128)(2,1)} %get-tuple-element.174.refs_0_), channel_id=1, source_target_pairs={{0,8},{8,16},{16,24},{24,0},{1,9},{9,17},{17,25},{25,1},{2,10},{10... | collective-permute-start | bytes 1277960 | tf_op jit(solution)/shard_map/ppermute | solution.py:380
  119.9 10.8 %collective-permute-start.14 = (bf16[4,208,256]{2,1,0:T(8,128)(2,1)}, bf16[4,208,256]{2,1,0:T(8,128)(2,1)S(1)}, u32[]{:S(2)}, u32[]{:S(2)}) collective-permute-start(bf16[4,208,256]{2,1,0:T(8,128)(2,1)} %get-tuple-element.174.refs_0_), channel_id=1, source_target_pairs={{0,24},{8,0},{16,8},{24,16},{1,25},{9,1},{17,9},{25,17},{2,26},{10... | collective-permute-start | bytes 1277960 | tf_op jit(solution)/shard_map/ppermute | solution.py:380
  120.0 13.3 %collective-permute-start.12 = (bf16[128,512]{1,0:T(8,128)(2,1)S(1)}, bf16[128,512]{1,0:T(8,128)(2,1)S(1)}, u32[]{:S(2)}, u32[]{:S(2)}) collective-permute-start(bf16[128,512]{1,0:T(8,128)(2,1)S(1)} %get-tuple-element.228), channel_id=1, source_target_pairs={{0,6},{2,0},{4,2},{6,4},{1,7},{3,1},{5,3},{7,5},{8,14},{10,8},{12,... | collective-permute-start | bytes 393224 | tf_op jit(solution)/shard_map/ppermute | solution.py:386
  120.9 12.6 %collective-permute-start.11 = (bf16[128,512]{1,0:T(8,128)(2,1)S(1)}, bf16[128,512]{1,0:T(8,128)(2,1)S(1)}, u32[]{:S(2)}, u32[]{:S(2)}) collective-permute-start(bf16[128,512]{1,0:T(8,128)(2,1)S(1)} %get-tuple-element.229), channel_id=1, source_target_pairs={{0,4},{2,6},{4,0},{6,2},{1,5},{3,7},{5,1},{7,3},{8,12},{10,14},{12... | collective-permute-start | bytes 393224 | tf_op jit(solution)/shard_map/ppermute | solution.py:386
  121.1 12.4 %collective-permute-start.10 = (bf16[128,512]{1,0:T(8,128)(2,1)S(1)}, bf16[128,512]{1,0:T(8,128)(2,1)S(1)}, u32[]{:S(2)}, u32[]{:S(2)}) collective-permute-start(bf16[128,512]{1,0:T(8,128)(2,1)S(1)} %get-tuple-element.230), channel_id=1, source_target_pairs={{0,2},{2,4},{4,6},{6,0},{1,3},{3,5},{5,7},{7,1},{8,10},{10,12},{12... | collective-permute-start | bytes 393224 | tf_op jit(solution)/shard_map/ppermute | solution.py:386
  128.7 11.0 %collective-permute-start.17 = (bf16[4,208,256]{2,1,0:T(8,128)(2,1)}, bf16[4,208,256]{2,1,0:T(8,128)(2,1)S(1)}, u32[]{:S(2)}, u32[]{:S(2)}) collective-permute-start(bf16[4,208,256]{2,1,0:T(8,128)(2,1)} %get-tuple-element.174.refs_0_), channel_id=1, source_target_pairs={{0,1},{1,0},{2,3},{3,2},{4,5},{5,4},{6,7},{7,6},{8,9},{9,8},{10,11... | collective-permute-start | bytes 1277960 | tf_op jit(solution)/shard_map/ppermute | solution.py:384
  130.7 6.0 %collective-permute-start.15 = (bf16[2,208,256]{2,1,0:T(8,128)(2,1)S(1)}, bf16[2,208,256]{2,1,0:T(8,128)(2,1)S(1)}, u32[]{:S(2)}, u32[]{:S(2)}) collective-permute-start(bf16[2,208,256]{2,1,0:T(8,128)(2,1)S(1)} %slice.118), channel_id=1, source_target_pairs={{0,8},{8,16},{16,24},{24,0},{1,9},{9,17},{17,25},{25,1},{2,10},{10... | collective-permute-start | bytes 638984 | tf_op jit(solution)/shard_map/ppermute | solution.py:382
  133.4 6.1 %collective-permute-start.16 = (bf16[2,208,256]{2,1,0:T(8,128)(2,1)S(1)}, bf16[2,208,256]{2,1,0:T(8,128)(2,1)S(1)}, u32[]{:S(2)}, u32[]{:S(2)}) collective-permute-start(bf16[2,208,256]{2,1,0:T(8,128)(2,1)S(1)} %slice.119), channel_id=1, source_target_pairs={{0,24},{8,0},{16,8},{24,16},{1,25},{9,1},{17,9},{25,17},{2,26},{10... | collective-permute-start | bytes 638984 | tf_op jit(solution)/shard_map/ppermute | solution.py:382
  133.5 6.2 %collective-permute-start.18 = (bf16[4,208,256]{2,1,0:T(8,128)(2,1)S(1)}, bf16[4,208,256]{2,1,0:T(8,128)(2,1)S(1)}, u32[]{:S(2)}, u32[]{:S(2)}) collective-permute-start(bf16[4,208,256]{2,1,0:T(8,128)(2,1)S(1)} %collective-permute-done.13.refs_1_), channel_id=1, source_target_pairs={{0,1},{1,0},{2,3},{3,2},{4,5},{5,4},{6,7},{7,6},{8,9},{9,8},{10,11... | collective-permute-start | bytes 1277960 | tf_op jit(solution)/shard_map/ppermute | solution.py:384
  133.6 6.1 %collective-permute-start.19 = (bf16[4,208,256]{2,1,0:T(8,128)(2,1)S(1)}, bf16[4,208,256]{2,1,0:T(8,128)(2,1)S(1)}, u32[]{:S(2)}, u32[]{:S(2)}) collective-permute-start(bf16[4,208,256]{2,1,0:T(8,128)(2,1)S(1)} %collective-permute-done.14.refs_2_), channel_id=1, source_target_pairs={{0,1},{1,0},{2,3},{3,2},{4,5},{5,4},{6,7},{7,6},{8,9},{9,8},{10,11... | collective-permute-start | bytes 1277960 | tf_op jit(solution)/shard_map/ppermute | solution.py:384
  136.7 2.9 %collective-permute-start.20 = (bf16[2,208,256]{2,1,0:T(8,128)(2,1)S(1)}, bf16[2,208,256]{2,1,0:T(8,128)(2,1)S(1)}, u32[]{:S(2)}, u32[]{:S(2)}) collective-permute-start(bf16[2,208,256]{2,1,0:T(8,128)(2,1)S(1)} %collective-permute-done.15.refs_3_), channel_id=1, source_target_pairs={{0,1},{1,0},{2,3},{3,2},{4,5},{5,4},{6,7},{7,6},{8,9},{9,8},{10,11... | collective-permute-start | bytes 638984 | tf_op jit(solution)/shard_map/ppermute | solution.py:384
  139.5 1.5 collective-permute-start.21
  163.0 9.6 %collective-permute-start.24 = (bf16[128,512]{1,0:T(8,128)(2,1)S(1)}, bf16[128,512]{1,0:T(8,128)(2,1)S(1)}, u32[]{:S(2)}, u32[]{:S(2)}) collective-permute-start(bf16[128,512]{1,0:T(8,128)(2,1)S(1)} %get-tuple-element.224), channel_id=1, source_target_pairs={{0,2},{2,4},{4,6},{6,0},{1,3},{3,5},{5,7},{7,1},{8,10},{10,12},{12... | collective-permute-start | bytes 393224 | tf_op jit(solution)/shard_map/ppermute | solution.py:396
  163.1 9.6 %collective-permute-start.23 = (bf16[128,512]{1,0:T(8,128)(2,1)S(1)}, bf16[128,512]{1,0:T(8,128)(2,1)S(1)}, u32[]{:S(2)}, u32[]{:S(2)}) collective-permute-start(bf16[128,512]{1,0:T(8,128)(2,1)S(1)} %get-tuple-element.225), channel_id=1, source_target_pairs={{0,4},{2,6},{4,0},{6,2},{1,5},{3,7},{5,1},{7,3},{8,12},{10,14},{12... | collective-permute-start | bytes 393224 | tf_op jit(solution)/shard_map/ppermute | solution.py:396
  163.7 9.6 %collective-permute-start.22 = (bf16[128,512]{1,0:T(8,128)(2,1)S(1)}, bf16[128,512]{1,0:T(8,128)(2,1)S(1)}, u32[]{:S(2)}, u32[]{:S(2)}) collective-permute-start(bf16[128,512]{1,0:T(8,128)(2,1)S(1)} %get-tuple-element.226), channel_id=1, source_target_pairs={{0,6},{2,0},{4,2},{6,4},{1,7},{3,1},{5,3},{7,5},{8,14},{10,8},{12,... | collective-permute-start | bytes 393224 | tf_op jit(solution)/shard_map/ppermute | solution.py:396
  (10 other events, 145.5 us)
Sparse Core Ops, SparseCore 0:
  9.6 63.9 all-gather.1
